TPU v7x, 32 devices: a whole 2x2x4 slice. The times are simulated.
32 devices in a mesh: dp: 4 (over z), bank: 4 (over y, x), head: 2 (over core).
Axes of the slice: x: 2, y: 2, z: 4, core: 2. Of those that a mesh axis runs over, the one named last changes fastest.
Arguments:
- feats: bfloat16 [2048, 2048], P('dp'), may hold values from -6 to 6
- w_first: bfloat16 [2048, 2048], P(None, ('bank', 'head')), may hold values from -0.125 to 0.125
- w_second: bfloat16 [2048, 256], P(('bank', 'head')), may hold values from -0.125 to 0.125
- fresh_keys: float32 [2048, 256], P('dp'), may hold values from -6 to 6
- bank: float32 [32768, 256], P(('bank', 'head'))
- block_lists: int32 [4, 32], P('dp'), may hold values from 0 to 63, as said below
- dest_rows: int32 [2048], P('dp'), may hold values from 0 to 32767, as said below
Outputs:
- loss: float32 [2048], P('dp')
- grad_first: float32 [2048, 2048], P('dp', ('bank', 'head'))
- grad_second: float32 [2048, 256], P(('bank', 'head'))
- new_bank: float32 [32768, 256], P(('bank', 'head'))
Inputs may be any that keep to these rules, and one draw needn't show every extreme that they name: `block_lists`: each row names 32 different blocks. `dest_rows`: all entries differ; the 512 entries of query block g name exactly 64 rows in each range of rows o * 4096 to (o + 1) * 4096 - 1.
All inputs are finite; a program needn't handle non-finite values.
Results may differ from a plain program's by a relative error of at most 0.012.
Values sent between devices are 32-bit elements; how exact they have to be, the bound alone decides.
A program may use at most 128 MiB of HBM per device.

v0:
```python
import jax
import jax.numpy as jnp
from jax import lax
from jax.sharding import PartitionSpec as P

BLOCK = 512


sharpness_divisor = 0.2
epsilon = 1e-06
lowest = -1e30


def joined(array, axis, combine):
    everything = jax.tree.map(lambda part: lax.all_gather(part, axis), array)
    leading = jax.tree.map(lambda part: part[0], everything)

    def hop(k, so_far):
        return combine(so_far, jax.tree.map(lambda part: part[k], everything))

    return lax.fori_loop(1, lax.axis_size(axis), hop, leading)


def unit_rows(values):
    norms = jnp.sqrt(jnp.sum(values * values, axis=1, keepdims=True) + epsilon)
    return (values / norms, norms)


def exact_scores(anchor_matrix, bank_entries):
    return (
        lax.dot_general(
            anchor_matrix,
            bank_entries,
            (((1,), (1,)), ((), ())),
            precision=lax.Precision.HIGHEST,
            preferred_element_type=jnp.float32,
        )
        / sharpness_divisor
    )


def join_stats(first, second):
    best = jnp.maximum(first[0], second[0])
    partition_total = first[1] * jnp.exp(first[0] - best) + second[1] * jnp.exp(second[0] - best)
    return (best, partition_total)


def shards(feats, w_first, w_second, fresh_keys, bank, block_lists, dest_rows):
    owner = lax.axis_index(("bank", "head"))
    owner_rows = bank.shape[0]
    hidden = jnp.maximum(jnp.dot(feats, w_first, preferred_element_type=jnp.float32), 0.0).astype(
        jnp.bfloat16
    )
    partial_embed = jnp.dot(hidden, w_second, preferred_element_type=jnp.float32)
    embed = lax.psum(partial_embed, ("bank", "head"))
    anchor_matrix, norms = unit_rows(embed)
    unit_length_bank, unused = unit_rows(fresh_keys)
    matching_similarity = jnp.sum(anchor_matrix * unit_length_bank, axis=1) / sharpness_divisor
    listed = block_lists[0]
    blocks_here = owner_rows // BLOCK
    owned = listed // blocks_here == owner
    owned_count = jnp.sum(owned.astype(jnp.int32))
    order = jnp.argsort(jnp.where(owned, 0, 1).astype(jnp.int32), stable=True)
    local_blocks = listed[order] - owner * blocks_here
    row_count = anchor_matrix.shape[0]

    def block_keys(index):
        return lax.dynamic_slice_in_dim(bank, local_blocks[index] * BLOCK, BLOCK, 0)

    start_best = jnp.full((row_count,), lowest, jnp.float32)
    start_total = jnp.zeros((row_count,), jnp.float32)
    start_weighted = jnp.zeros((row_count, anchor_matrix.shape[1]), jnp.float32)

    def first_pass(index, carry):
        best, partition_total = carry
        similarity_matrix = exact_scores(anchor_matrix, block_keys(index))
        new_best = jnp.maximum(best, jnp.max(similarity_matrix, axis=1))
        partition_total = partition_total * jnp.exp(best - new_best) + jnp.sum(
            jnp.exp(similarity_matrix - new_best[:, None]), axis=1
        )
        return (new_best, partition_total)

    local_stats = lax.fori_loop(0, owned_count, first_pass, (start_best, start_total))
    neg_best, neg_total = joined(local_stats, ("bank", "head"), join_stats)
    best = jnp.maximum(neg_best, matching_similarity)
    positive_weight = jnp.exp(matching_similarity - best)
    partition_total = neg_total * jnp.exp(neg_best - best) + positive_weight

    def second_pass(index, probability_mixed_bank):
        bank_entries = block_keys(index)
        shares = (
            jnp.exp(exact_scores(anchor_matrix, bank_entries) - best[:, None])
            / partition_total[:, None]
        )
        return probability_mixed_bank + jnp.dot(
            shares,
            bank_entries,
            precision=lax.Precision.HIGHEST,
            preferred_element_type=jnp.float32,
        )

    local_weighted = lax.fori_loop(0, owned_count, second_pass, start_weighted)
    probability_mixed_bank = lax.psum(local_weighted, ("bank", "head"))
    loss = best + jnp.log(partition_total) - matching_similarity
    anchor_derivative = (
        probability_mixed_bank
        + (positive_weight / partition_total - 1.0)[:, None] * unit_length_bank
    ) / sharpness_divisor
    inner = jnp.sum(anchor_matrix * anchor_derivative, axis=1, keepdims=True)
    grad_z = ((anchor_derivative - anchor_matrix * inner) / norms).astype(jnp.bfloat16)
    second_part = lax.dot_general(
        hidden, grad_z, (((0,), (0,)), ((), ())), preferred_element_type=jnp.float32
    )
    grad_second = lax.psum(second_part, "dp")
    grad_hidden = lax.dot_general(
        grad_z, w_second, (((1,), (1,)), ((), ())), preferred_element_type=jnp.float32
    )
    grad_pre = jnp.where(hidden > 0, grad_hidden, 0.0).astype(jnp.bfloat16)
    grad_first = lax.psum_scatter(
        lax.dot_general(
            feats, grad_pre, (((0,), (0,)), ((), ())), preferred_element_type=jnp.float32
        ),
        "dp",
        scatter_dimension=0,
        tiled=True,
    )
    got_keys, got_dest = (
        lax.all_gather(unit_length_bank, "dp", axis=0, tiled=True),
        lax.all_gather(dest_rows.astype(jnp.float32), "dp", axis=0, tiled=True),
    )
    local_rows = got_dest.astype(jnp.int32) - owner * owner_rows
    inside = (local_rows >= 0) & (local_rows < owner_rows)
    new_bank = bank.at[jnp.where(inside, local_rows, owner_rows)].set(got_keys, mode="drop")
    return (loss, grad_first, grad_second, new_bank)


def solution(mesh):
    return jax.shard_map(
        shards,
        mesh=mesh,
        in_specs=(
            P("dp", None),
            P(None, ("bank", "head")),
            P(("bank", "head"), None),
            P("dp", None),
            P(("bank", "head"), None),
            P("dp", None),
            P("dp"),
        ),
        out_specs=(
            P("dp"),
            P("dp", ("bank", "head")),
            P(("bank", "head"), None),
            P(("bank", "head"), None),
        ),
        check_vma=False,
    )
```

profile of v0, /device:TPU:0, one launch (start us, length us, event | category | flops | bytes accessed | tf_op | source)
XLA Modules:
  0.0 383.8 jit_solution(11246029741084995186)
XLA Ops:
  7.2 4.6 %copy.49 = f32[4096,256]{1,0:T(8,128)} copy(f32[4096,256]{1,0:T(8,128)} %param.17) | data formatting | bytes 8388608
  11.9 0.7 fusion.9
  12.8 1.0 fusion.18
  13.9 1.6 sort.17
  15.5 0.7 gather_fusion
  16.2 0.7 fusion.14
  17.1 54.1 %all-reduce.4.cloned.1.call-done = f32[512,256]{1,0:T(8,128)} async-done(((f32[512,256]{1,0:T(8,128)}), f32[512,256]{1,0:T(8,128)}) %all-reduce.4.cloned.1.call-update) | async-done | bytes 524304 | tf_op jit(solution)/shard_map/psum | solution.py:55
  71.2 1.2 multiply_reduce_fusion.3
  72.5 2.0 multiply_reduce_fusion.1
  74.5 13.9 %while.39 = (s32[]{:T(128)}, f32[512]{0:T(512)S(1)}, f32[512]{0:T(512)S(1)}, s32[]{:T(128)}, s32[32]{0:T(128)S(1)}, /*index=5*/f32[4096,256]{1,0:T(8,128)}, f32[...) while((s32[]{:T(128)}, f32[512]{0:T(512)S(1)}, ...), condition=%wide.region_7.8_spmd, body=%wide.region_4.0_spmd.sunk | while | flops 806355968 | bytes 3172573 | solution.py:83
  75.2 0.7 dynamic_slice.49
  76.6 2.1 fusion.40
  78.7 0.2 exponential_reduce_fusion.2
  79.6 0.7 dynamic_slice.49
  81.0 2.1 fusion.40
  83.1 0.2 exponential_reduce_fusion.2
  84.0 0.7 dynamic_slice.49
  85.4 2.1 fusion.40
  87.5 0.2 exponential_reduce_fusion.2
  88.5 30.2 %all-gather.2 = f32[8,1,512]{2,1,0:T(1,128)S(1)} all-gather(f32[1,1,512]{2,1,0:T(1,128)S(1)} %bitcast.49), channel_id=2, replica_groups=mesh['dp'=4,'bank'=4,'head'=2] {'bank','head'}, dimensions={0}, use_global_device_ids=true | all-gather | bytes 18432 | tf_op jit(solution)/shard_map/all_gather | solution.py:15
  118.7 7.7 %all-gather.3 = f32[8,1,512]{2,1,0:T(1,128)S(1)} all-gather(f32[1,1,512]{2,1,0:T(1,128)S(1)} %bitcast.52), channel_id=3, replica_groups=mesh['dp'=4,'bank'=4,'head'=2] {'bank','head'}, dimensions={0}, use_global_device_ids=true | all-gather | bytes 18432 | tf_op jit(solution)/shard_map/all_gather | solution.py:15
  126.4 0.4 while.40
  126.7 0.6 divide_add_fusion
  127.4 23.8 %while.41 = (s32[]{:T(128)}, f32[512,256]{1,0:T(8,128)S(1)}, s32[]{:T(128)}, s32[32]{0:T(128)}, f32[4096,256]{1,0:T(8,128)}, /*index=5*/f32[512,256]{1,0:T(8,128...) while((s32[]{:T(128)}, f32[512,256]{1,0:T(8,128)S(1)}, ...), condition=%wide.region_13.14_spmd, body=%wide.region_12.13_spmd.sunk | while | flops 1611530240 | bytes 4722921 | solution.py:102
  128.1 1.3 dynamic_slice.53
  129.9 2.2 fusion.45
  132.1 3.0 convolution_add_fusion.2
  135.8 1.3 dynamic_slice.53
  137.6 2.2 fusion.45
  139.8 3.0 convolution_add_fusion.2
  143.5 1.3 dynamic_slice.53
  145.4 2.2 fusion.45
  147.6 3.0 convolution_add_fusion.2
  151.2 0.8 copy-done.2
  152.1 0.7 all-gather.7.cloned.1.call-update
  152.9 92.7 %all-reduce.6.cloned.1.call-done = f32[512,256]{1,0:T(8,128)} async-done(((f32[512,256]{1,0:T(8,128)}), f32[512,256]{1,0:T(8,128)}) %all-reduce.6.cloned.1.call-update) | async-done | bytes 524304 | tf_op jit(solution)/shard_map/psum | solution.py:103
  245.6 1.4 multiply_reduce_fusion
  247.0 2.0 divide_convert_fusion
  249.0 3.3 convolution_bitcast_fusion
  252.4 0.6 copy-done.7
  253.0 12.1 %all-gather.4 = f32[4,1,512]{2,1,0:T(1,128)S(1)} all-gather(f32[1,1,512]{2,1,0:T(1,128)S(1)} %bitcast.58), channel_id=1, replica_groups=mesh['dp'=4,'bank'=4,'head'=2] {'dp'}, dimensions={0}, use_global_device_ids=true | all-gather | bytes 10240 | tf_op jit(solution)/shard_map/all_gather | solution.py:129
  265.1 1.0 fusion.19
  266.2 27.0 %all-gather.7.cloned.1.call-done = f32[2048,256]{1,0:T(8,128)} async-done(((f32[512,256]{1,0:T(8,128)}), f32[2048,256]{1,0:T(8,128)}) %all-gather.7.cloned.1.call-update) | async-done | bytes 2097168 | tf_op jit(solution)/shard_map/all_gather | solution.py:128
  293.1 13.6 %scatter_fusion = f32[4096,256]{1,0:T(8,128)} fusion(f32[4096,256]{1,0:T(8,128)} %get-tuple-element.541, s32[2048]{0:T(1024)S(1)} %compare_select_fusion, f32[2048,256]{1,0:T(8,128)} %all-gather.7.cloned.1.call-done), kind=kCustom, calls=%fused_computation.1 | custom fusion | bytes 6299648 | tf_op jit(solution)/shard_map/scatter | solution.py:133
  306.7 31.3 %reduce-scatter.2.cloned.1.call-done = f32[512,256]{0,1:T(8,128)} async-done(((f32[2048,256]{0,1:T(8,128)}), f32[512,256]{0,1:T(8,128)}) %reduce-scatter.2.cloned.1.call-update) | async-done | bytes 524304 | tf_op jit(solution)/shard_map/reduce_scatter | solution.py:119
  338.1 2.0 copy.13
  340.1 35.5 %all-reduce.8.cloned.1.call-done = f32[256,256]{1,0:T(8,128)} async-done(((f32[256,256]{1,0:T(8,128)}), f32[256,256]{1,0:T(8,128)}) %all-reduce.8.cloned.1.call-update) | async-done | bytes 262160 | tf_op jit(solution)/shard_map/psum | solution.py:114
  375.6 1.7 copy.50
  (67 shorter events, 1.0 us)
Async XLA Ops:
  7.2 4.7 %copy-start = (bf16[512,2048]{1,0:T(8,128)(2,1)S(1)}, bf16[512,2048]{1,0:T(8,128)(2,1)}, u32[]{:S(2)}) copy-start(bf16[512,2048]{1,0:T(8,128)(2,1)} %param.13) | copy-start | bytes 6291460
  7.2 64.1 %all-reduce.4.cloned.1.call-start = ((), (), s32[]{:S(2)}) async-start(), calls=%async_computation.1 | async-start | bytes 1048576 | tf_op jit(solution)/shard_map/psum | solution.py:55
  7.2 4.6 %copy-start.9 = (bf16[2048,256]{1,0:T(8,128)(2,1)S(1)}, bf16[2048,256]{1,0:T(8,128)(2,1)}, u32[]{:S(2)}) copy-start(bf16[2048,256]{1,0:T(8,128)(2,1)} %param.14) | copy-start | bytes 3145732
  11.9 0.9 copy-start.6
  11.9 2.0 copy-start.1
  11.9 5.1 %copy-start.5 = (f32[512,256]{1,0:T(8,128)S(1)}, f32[512,256]{1,0:T(8,128)}, u32[]{:S(2)}) copy-start(f32[512,256]{1,0:T(8,128)} %param.16) | copy-start | bytes 1572868
  13.8 231.8 %all-reduce.6.cloned.1.call-start = ((), (), s32[]{:S(2)}) async-start(), calls=%async_computation.2 | async-start | bytes 1048576 | tf_op jit(solution)/shard_map/psum | solution.py:103
  88.4 38.3 %copy-start.8 = (s32[32]{0:T(128)}, s32[32]{0:T(128)S(1)}, u32[]{:S(2)}) copy-start(s32[32]{0:T(128)S(1)} %get-tuple-element.559) | copy-start | bytes 388
  151.2 0.8 copy-start.2
  152.1 95.0 %copy-start.3 = (f32[512,256]{1,0:T(8,128)S(1)}, f32[512,256]{1,0:T(8,128)}, u32[]{:S(2)}) copy-start(f32[512,256]{1,0:T(8,128)} %get-tuple-element.283) | copy-start | bytes 1572868
  152.1 141.1 %all-gather.7.cloned.1.call-start = ((), (), s32[]{:S(2)}) async-start(), calls=%async_computation.5 | async-start | bytes 2621440 | tf_op jit(solution)/shard_map/all_gather | solution.py:128
  152.8 185.3 %reduce-scatter.2.cloned.1.call-start = ((), (), s32[]{:S(2)}) async-start(), calls=%async_computation.3 | async-start | bytes 2621440 | tf_op jit(solution)/shard_map/reduce_scatter | solution.py:119
  252.4 0.7 copy-start.7
  252.4 12.8 %copy-start.4 = (bf16[512,256]{1,0:T(8,128)(2,1)S(1)}, bf16[512,256]{1,0:T(8,128)(2,1)}, u32[]{:S(2)}) copy-start(bf16[512,256]{1,0:T(8,128)(2,1)} %divide_convert_fusion) | copy-start | bytes 786436
  252.4 123.3 %all-reduce.8.cloned.1.call-start = ((), (), s32[]{:S(2)}) async-start(), calls=%async_computation.4 | async-start | bytes 524288 | tf_op jit(solution)/shard_map/psum | solution.py:114
Sparse Core Ops, SparseCore 0:
  13.9 57.2 all-reduce.3
  152.2 93.3 all-reduce.5
  247.7 45.3 all-gather.6
  295.3 42.7 reduce-scatter.1
  340.9 34.6 all-reduce.7
where the time goes:
time: 386 us; the launch traced here: 384 us
  waiting for transfers between devices  241 us (62%)
  blocking collectives  50 us (13%)
  local copies, waits for them, and re-layouts  30.2 us (8%)
  matrix products  27.8 us (7%)
  between operations  14 us (4%)
  other arithmetic  10.6 us (3%)
  loops' own time  9.7 us (3%)
    psum x1, waiting for transfers between devices, shards(): probability_mixed_bank = lax.psum(local_weighted, ('bank', 'head'))  92.7 us
    psum x1, waiting for transfers between devices, shards(): embed = lax.psum(partial_embed, ('bank', 'head'))  54.1 us
    all_gather x2, blocking collectives, joined(): everything = jax.tree.map(lambda part: lax.all_gather(part, axis), array)  37.9 us
    psum x1, waiting for transfers between devices, shards(): grad_second = lax.psum(second_part, 'dp')  35.5 us
    reduce_scatter x1, waiting for transfers between devices, shards(): lax.psum_scatter(lax.dot_general(feats, grad_pre, (((0,), (0,)), ((), ())...  31.3 us
    all_gather x1, waiting for transfers between devices, shards(): lax.all_gather(unit_length_bank, 'dp', axis=0, tiled=True)  27 us
    scatter x1, local copies, waits for them, and re-layouts, shards(): bank.at[jnp.where(inside, local_rows, owner_rows)]  13.6 us
    dot_general x6, matrix products, exact_scores(): lax.dot_general(anchor_matrix, bank_entries, (((1,), (1,)), ((), ())), pr...  12.9 us
  transfers between devices with their start and end apart: 5, of which 5 were waited for; matrix products, arithmetic and copies ran while one was open for 7% of the time, Pallas kernels for 0%

commit v1 on v0

v1 whole, which is shorter than its diff:
```python
import functools
import math

import jax
import jax.numpy as jnp
from jax import lax
from jax.experimental import pallas as pl
from jax.experimental.pallas import tpu as pltpu
from jax.sharding import PartitionSpec as P

BLOCK = 512
EPS = 1e-6
SCALE = 5.0
LOG2E = 1.4426950408889634
LN2 = 0.6931471805599453
LOWEST = -1e30
MESH = pl.DeviceIdType.MESH
F32 = jnp.float32
BF16 = jnp.bfloat16


def nt(a, b, **kw):
    return lax.dot_general(a, b, (((1,), (1,)), ((), ())), preferred_element_type=F32, **kw)


def tn(a, b):
    return lax.dot_general(a, b, (((0,), (0,)), ((), ())), preferred_element_type=F32)


def body(
    D, N, H,
    feats, w1, w2, fresh, bank, bias, dest,
    loss_out, gf_out, gs_out, keys_out, kd_out,
    hid, zp, zr, zs, zfull, kcat, qcat, sbuf, acc, ml, ar, mr, st, gz, gfull, lt, lr,
    gfs, gfr, gsp, gsr, gst, gsf, ks, kr, kd, kdr,
    s_z, r_z, s_q, r_q, s_a, r_a, s_m, r_m, s_g, r_g, s_l, r_l,
    s_f, r_f, s_s, r_s, s_t, r_t, s_k, r_k, s_d, r_d,
):
    d = lax.axis_index("dp")
    bk = lax.axis_index("bank")
    hd = lax.axis_index("head")
    me = bk * H + hd
    rows = zp.shape[0]
    R = rows // N
    nblk = kcat.shape[0]

    def plane(k):
        p = lax.rem(me + k, N)
        return p, {"bank": lax.div(p, H), "head": lax.rem(p, H)}

    def line(j):
        p = lax.rem(d + j, D)
        return p, {"dp": p}

    def chunk(p, size):
        return pl.ds(pl.multiple_of(p * size, size), size)

    def send(src, dst, ss, rs, dev):
        c = pltpu.make_async_remote_copy(
            src_ref=src, dst_ref=dst, send_sem=ss, recv_sem=rs,
            device_id=dev, device_id_type=MESH)
        c.start()
        return c

    barrier = pltpu.get_barrier_semaphore()
    for k in range(1, N):
        pl.semaphore_signal(barrier, inc=1, device_id=plane(k)[1], device_id_type=MESH)
    for j in range(1, D):
        pl.semaphore_signal(barrier, inc=1, device_id=line(j)[1], device_id_type=MESH)

    h = jnp.maximum(jnp.dot(feats[...], w1[...], preferred_element_type=F32), 0.0).astype(BF16)
    hid[...] = h
    zp[...] = jnp.dot(h, w2[...], preferred_element_type=F32)
    pl.semaphore_wait(barrier, N - 1 + D - 1)

    pending = []
    z_copies = []
    for k in range(1, N):
        p, dev = plane(k)
        z_copies.append(send(zp.at[chunk(p, R)], zr.at[k], s_z.at[k], r_z.at[k], dev))

    f = fresh[...]
    unit = f / jnp.sqrt(jnp.sum(f * f, axis=1, keepdims=True) + EPS)
    local = dest[...] - (me * bank.shape[0]).astype(F32)
    inside = (local >= 0.0) & (local < float(bank.shape[0]))
    one = jnp.where(inside, 1.0, 0.0)
    upper = lax.broadcasted_iota(jnp.int32, (rows, rows), 0) <= lax.broadcasted_iota(
        jnp.int32, (rows, rows), 1)
    place = jnp.dot(one.astype(BF16), jnp.where(upper, 1.0, 0.0).astype(BF16),
                    preferred_element_type=F32) * one
    want = lax.broadcasted_iota(jnp.int32, (128, rows), 0).astype(F32) + 1.0
    pick = jnp.where(want == jnp.broadcast_to(place[0:1, :], (128, rows)), 1.0, 0.0)
    ks[...] = jnp.dot(pick[0:R], unit, precision=lax.Precision.HIGHEST, preferred_element_type=F32)
    kd[...] = nt(jnp.where(inside, local, 0.0), pick, precision=lax.Precision.HIGHEST)
    for j in range(1, D):
        dev = line(j)[1]
        pending.append(send(ks, kr.at[j], s_k.at[j], r_k.at[j], dev))
        pending.append(send(kd, kdr.at[j], s_d.at[j], r_d.at[j], dev))
    kr[0] = ks[...]
    kdr[0] = kd[...]

    def split(b, carry):
        x = bank[pl.ds(pl.multiple_of(b * BLOCK, BLOCK), BLOCK), :]
        hi = x.astype(BF16)
        lo = (x - hi.astype(F32)).astype(BF16)
        kcat[b, :, 0:256] = hi
        kcat[b, :, 256:512] = lo
        kcat[b, :, 512:768] = hi
        return carry

    lax.fori_loop(0, nblk, split, 0)

    total_z = zp[chunk(me, R), :]
    for k in range(1, N):
        z_copies[k - 1].wait_recv()
        total_z = total_z + zr[k]
    zs[...] = total_z
    zfull[chunk(me, R), :] = total_z
    q_copies = []
    for k in range(1, N):
        dev = plane(k)[1]
        q_copies.append(send(zs, zfull.at[chunk(me, R)], s_q.at[k], r_q.at[k], dev))
    for c in q_copies:
        c.wait_recv()
    z = zfull[...]
    q = z / jnp.sqrt(jnp.sum(z * z, axis=1, keepdims=True) + EPS) * (SCALE * LOG2E)
    qh = q.astype(BF16)
    qcat[:, 0:256] = qh
    qcat[:, 256:512] = qh
    qcat[:, 512:768] = (q - qh.astype(F32)).astype(BF16)

    def scores(b, best):
        s = nt(qcat[...], kcat[b]) + bias[b]
        sbuf[b] = s
        for t in range(BLOCK // 128):
            best = jnp.maximum(best, s[:, t * 128:(t + 1) * 128])
        return best

    best = lax.fori_loop(0, nblk, scores, jnp.full((rows, 128), LOWEST, F32))
    best = jnp.max(best, axis=1, keepdims=True)
    acc[...] = jnp.zeros_like(acc)

    def mix(b, total):
        w = jnp.exp2(sbuf[b] - best)
        for t in range(BLOCK // 128):
            total = total + w[:, t * 128:(t + 1) * 128]
        both = jnp.dot(w.astype(BF16), kcat[b, :, 0:512], preferred_element_type=F32)
        acc[...] += both[:, 0:256] + both[:, 256:512]
        return total

    total = lax.fori_loop(0, nblk, mix, jnp.zeros((rows, 128), F32))
    total = jnp.sum(total, axis=1, keepdims=True)
    lane = lax.broadcasted_iota(jnp.int32, (rows, 128), 1)
    stat = jnp.where(lane == 0, best, total).T
    for c in range(rows // 128):
        ml[c] = stat[0:8, c * 128:(c + 1) * 128]

    a_copies = []
    per = 128 // R
    for k in range(1, N):
        p, dev = plane(k)
        a_copies.append(send(ml.at[lax.div(p, per)], mr.at[k], s_m.at[k], r_m.at[k], dev))
        a_copies.append(send(acc.at[chunk(p, R)], ar.at[k], s_a.at[k], r_a.at[k], dev))
    mr[0] = ml[lax.div(me, per)]
    for c in a_copies:
        c.wait_recv()
    tiles = mr[...].reshape(N * 8, 128)
    st[...] = jnp.concatenate([tiles, jnp.zeros((128 - N * 8, 128), F32)], axis=0).T
    stats = st[chunk(lax.rem(me, per), R), :]

    zc = zfull[chunk(me, R), :]
    norm = jnp.sqrt(jnp.sum(zc * zc, axis=1, keepdims=True) + EPS)
    qc = zc / norm
    fc = fresh[chunk(me, R), :]
    uc = fc / jnp.sqrt(jnp.sum(fc * fc, axis=1, keepdims=True) + EPS)
    pos = jnp.sum(qc * uc, axis=1, keepdims=True) * (SCALE * LOG2E)
    top = pos
    for k in range(N):
        top = jnp.maximum(top, stats[:, k * 8:k * 8 + 1])
    pw = jnp.exp2(pos - top)
    den = pw
    mixed = jnp.zeros((R, acc.shape[1]), F32)
    for k in range(N):
        wk = jnp.exp2(stats[:, k * 8:k * 8 + 1] - top)
        den = den + wk * stats[:, k * 8 + 1:k * 8 + 2]
        mixed = mixed + wk * (acc[chunk(me, R), :] if k == 0 else ar[k])
    losses = (top - pos) * LN2 + jnp.log(den)
    gq = (mixed / den + (pw / den - 1.0) * uc) * SCALE
    inner = jnp.sum(qc * gq, axis=1, keepdims=True)
    g = ((gq - qc * inner) / norm).astype(BF16).astype(F32)
    gz[...] = g
    gfull[chunk(me, R), :] = g
    wide = jnp.concatenate(
        [jnp.broadcast_to(losses, (R, 128)), jnp.zeros((128 - R, 128), F32)], axis=0)
    lt[...] = wide.T[0:8, :]
    lr[me] = lt[...]
    g_copies = []
    for k in range(1, N):
        dev = plane(k)[1]
        g_copies.append(send(gz, gfull.at[chunk(me, R)], s_g.at[k], r_g.at[k], dev))
        pending.append(send(lt, lr.at[me], s_l.at[k], r_l.at[k], dev))
    for c in g_copies:
        c.wait_recv()

    gb = gfull[...].astype(BF16)
    gsp[...] = tn(hid[...], gb)
    S = gsp.shape[0] // D
    s_copies = []
    for j in range(1, D):
        p, dev = line(j)
        s_copies.append(send(gsp.at[chunk(p, S)], gsr.at[j], s_s.at[j], r_s.at[j], dev))
    gp = nt(gb, w2[...])
    gp = jnp.where(hid[...] > 0, gp, 0.0).astype(BF16)
    F = gf_out.shape[0]
    f_copies = []
    if F % 128:
        for t in range(feats.shape[1] // 256):
            gfs[t * 256:(t + 1) * 256, :] = tn(feats[:, t * 256:(t + 1) * 256], gp)
    for j in [*range(1, D), 0]:
        p, dev = line(j)
        if F % 128 == 0:
            gfs[chunk(p, F), :] = tn(feats[:, chunk(p, F)], gp)
        if j:
            f_copies.append(send(gfs.at[chunk(p, F)], gfr.at[j], s_f.at[j], r_f.at[j], dev))

    total_s = gsp[chunk(d, S), :]
    for j in range(1, D):
        s_copies[j - 1].wait_recv()
        total_s = total_s + gsr[j]
    gst[...] = total_s
    gsf[chunk(d, S), :] = total_s
    t_copies = []
    for j in range(1, D):
        dev = line(j)[1]
        t_copies.append(send(gst, gsf.at[chunk(d, S)], s_t.at[j], r_t.at[j], dev))

    for c in pending:
        c.wait_recv()
    keys_out[...] = kr[...].reshape(keys_out.shape)
    kd_out[...] = kdr[...]
    loss_out[...] = lr[...]
    for c in t_copies:
        c.wait_recv()
    gs_out[...] = gsf[...]
    gf_out[...] = gfs[chunk(d, F), :]
    for j in range(1, D):
        f_copies[j - 1].wait_recv()
        gf_out[...] += gfr[j]
    for c in z_copies + q_copies + a_copies + g_copies + s_copies + t_copies + f_copies + pending:
        c.wait_send()


def shards(D, N, H, feats, w_first, w_second, fresh_keys, bank, block_lists, dest_rows):
    owner = lax.axis_index(("bank", "head"))
    rows, din = feats.shape
    hcols = w_first.shape[1]
    E = w_second.shape[1]
    nblk = bank.shape[0] // BLOCK
    R = rows // N
    F = din // D
    S = hcols // D
    mine = owner * nblk + jnp.arange(nblk, dtype=jnp.int32)
    owned = jnp.any(block_lists[0][None, :] == mine[:, None], axis=1)
    bias = jnp.where(owned, 0.0, LOWEST).astype(F32)
    dest = jnp.broadcast_to(dest_rows.astype(F32)[None, :], (8, rows))
    V = pl.BlockSpec(memory_space=pltpu.VMEM)
    sds = jax.ShapeDtypeStruct
    vm = pltpu.VMEM
    scratch = [
        vm((rows, hcols), BF16), vm((rows, E), F32), vm((N, R, E), F32), vm((R, E), F32),
        vm((rows, E), F32), vm((nblk, BLOCK, 3 * E), BF16), vm((rows, 3 * E), BF16),
        vm((nblk, rows, BLOCK), F32), vm((rows, E), F32), vm((rows // 128, 8, 128), F32),
        vm((N, R, E), F32), vm((N, 8, 128), F32), vm((128, 128), F32), vm((R, E), F32),
        vm((rows, E), F32), vm((8, 128), F32), vm((N, 8, 128), F32),
        vm((din, hcols), F32), vm((D, F, hcols), F32), vm((hcols, E), F32), vm((D, S, E), F32),
        vm((S, E), F32), vm((hcols, E), F32), vm((R, E), F32), vm((D, R, E), F32),
        vm((8, 128), F32), vm((D, 8, 128), F32),
    ]
    dma = pltpu.SemaphoreType.DMA
    sems = [dma((N,))] * 12 + [dma((D,))] * 10
    loss, grad_first, grad_second, keys, kdest = pl.pallas_call(
        functools.partial(body, D, N, H),
        out_shape=(
            sds((N, 8, 128), F32), sds((F, hcols), F32), sds((hcols, E), F32),
            sds((D * R, E), F32), sds((D, 8, 128), F32),
        ),
        in_specs=[V, V, V, V, V, pl.BlockSpec(memory_space=pltpu.SMEM), V],
        out_specs=(V,) * 5,
        scratch_shapes=scratch + sems,
        compiler_params=pltpu.CompilerParams(
            collective_id=0, has_side_effects=True, vmem_limit_bytes=56 * 1024 * 1024),
    )(feats, w_first, w_second, fresh_keys, bank, bias, dest)
    index = jnp.round(kdest[:, 0, :R]).astype(jnp.int32).reshape(D * R)
    new_bank = bank.at[index].set(keys, unique_indices=True, mode="promise_in_bounds")
    return (loss[:, 0, :R].reshape(rows), grad_first, grad_second, new_bank)


def solution(mesh):
    D = mesh.shape["dp"]
    H = mesh.shape["head"]
    N = mesh.shape["bank"] * H
    return jax.shard_map(
        functools.partial(shards, D, N, H),
        mesh=mesh,
        in_specs=(
            P("dp", None),
            P(None, ("bank", "head")),
            P(("bank", "head"), None),
            P("dp", None),
            P(("bank", "head"), None),
            P("dp", None),
            P("dp"),
        ),
        out_specs=(
            P("dp"),
            P("dp", ("bank", "head")),
            P(("bank", "head"), None),
            P(("bank", "head"), None),
        ),
        check_vma=False,
    )
```

time: 386 us -> 125 us (0.32)
  waiting for transfers between devices: 241 us -> 0 us
  Pallas kernels: 0 us -> 108 us
  blocking collectives: 50 us -> 0 us
  matrix products: 27.8 us -> 0 us
  local copies, waits for them, and re-layouts: 30.2 us -> 14.2 us
  between operations: 14 us -> 0.68 us
  loops' own time: 9.7 us -> 0 us
  other arithmetic: 10.6 us -> 1.45 us
    psum x3 -> x0, waiting for transfers between devices: 182 us -> none  [the longest x1 92.7 us: shards(): probability_mixed_bank = lax.psum(local_weighted, ('bank', 'head'))]
    pallas_call x0 -> x1, Pallas kernels: none -> 108 us  [shards(): pl.pallas_call(functools.partial(body, D, N, H), out_shape=(sds((N, 8, 12...]
    all_gather x3 -> x0, blocking collectives: 50 us -> none  [the longest x2 37.9 us: joined(): everything = jax.tree.map(lambda part: lax.all_gather(part, axis), array)]
    reduce_scatter x1 -> x0, waiting for transfers between devices: 31.3 us -> none  [shards(): lax.psum_scatter(lax.dot_general(feats, grad_pre, (((0,), (0,)), ((), ())...]
    dot_general x13 -> x0, matrix products: 27.8 us -> none  [the longest x6 12.9 us: exact_scores(): lax.dot_general(anchor_matrix, bank_entries, (((1,), (1,)), ((), ())), pr...]
    all_gather x1 -> x0, waiting for transfers between devices: 27 us -> none  [shards(): lax.all_gather(unit_length_bank, 'dp', axis=0, tiled=True)]
    another operation x3 -> x0, loops' own time: 9.7 us -> none  [the longest x1 4.98 us: shards(): lax.fori_loop(0, owned_count, first_pass, (start_best, start_total))]
    scatter x1, local copies, waits for them, and re-layouts: 13.6 us -> 5.98 us  [shards(): bank.at[index].set(keys, unique_indices=True, mode='promise_in_bounds')]
  transfers between devices with their start and end apart: 5 -> 0, of which waited for: 5 -> 0; matrix products, arithmetic and copies ran while one was open for 7% -> 0% of each run, Pallas kernels for 0% -> 0%
where the time goes in v1:
time: 125 us; the launch traced here: 124 us
  Pallas kernels  108 us (86%)
  local copies, waits for them, and re-layouts  14.2 us (11%)
  other arithmetic  1.45 us (1%)
    pallas_call x1, Pallas kernels, shards(): pl.pallas_call(functools.partial(body, D, N, H), out_shape=(sds((N, 8, 12...  108 us
    unnamed x11, local copies, waits for them, and re-layouts  5.99 us
    scatter x1, local copies, waits for them, and re-layouts, shards(): bank.at[index].set(keys, unique_indices=True, mode='promise_in_bounds')  5.98 us

profile of v1, /device:TPU:0, one launch (start us, length us, event | category | flops | bytes accessed | tf_op | source)
XLA Modules:
  0.0 124.3 jit_solution(9943943250515125639)
XLA Ops:
  0.6 0.0 copy-start.3
  0.6 0.0 copy-start.2
  0.7 4.5 %copy.15.bank = f32[4096,256]{1,0:T(8,128)} copy(f32[4096,256]{1,0:T(8,128)} %param.11) | data formatting | bytes 8388608
  5.1 0.0 copy-done.3
  5.1 0.2 compare_reduce_fusion
  5.3 0.5 broadcast_select_fusion.bias
  5.8 0.0 copy-done.2
  5.8 0.6 broadcast_in_dim.18.dest
  6.5 108.0 %shard_map.102 = (f32[8,8,128]{2,1,0:T(8,128)}, f32[512,256]{1,0:T(8,128)}, f32[256,256]{1,0:T(8,128)}, f32[256,256]{1,0:T(8,128)}, f32[4,8,128]{2,1,0:T(8,128)}) custom-call(bf16[512,2048]{1,0:T(8,128)(2,1)} %feats.1, bf16[2048,256]{1,0:T(8,128)(2,1)} %w1.1, bf16[256,256]{1,0:T(8,128)(2,1)} %w2.1, f32[512,256]{1,0:T(8,128)} %fresh.1, ...), custom_call_target="tpu_custom_call" | custom-call | tf_op jit(solution)/shard_map/pallas_call | solution.py:281
  114.4 0.0 copy-start
  114.4 0.0 copy-start.1
  114.5 0.8 slice_reduce_fusion
  115.3 0.7 reshape_squeeze.3
  116.0 0.7 convert_reduce_fusion
  116.7 0.1 convert_element_type.19
  116.8 6.0 %scatter_fusion = f32[4096,256]{1,0:T(8,128)} fusion(f32[4096,256]{1,0:T(8,128)} %copy.15.bank, s32[256]{0:T(256)S(1)} %bitcast.3, f32[256,256]{1,0:T(8,128)} %get-tuple-element.13), kind=kCustom, calls=%fused_computation | custom fusion | bytes 787456 | tf_op jit(solution)/shard_map/scatter | solution.py:294
  122.8 0.0 copy-done
  122.8 0.8 copy.16
  123.6 0.0 copy-done.1
  123.6 0.7 copy.17
  (3 shorter events, 0.0 us)
Async XLA Ops:
  0.6 4.5 %copy-start.3 = (s32[1,32]{1,0:T(1,128)S(1)}, s32[1,32]{1,0:T(1,128)}, u32[]{:S(2)}) copy-start(s32[1,32]{1,0:T(1,128)} %param.12) | copy-start | bytes 388
  0.6 5.2 %copy-start.2 = (s32[512]{0:T(512)S(1)}, s32[512]{0:T(512)}, u32[]{:S(2)}) copy-start(s32[512]{0:T(512)} %param.13) | copy-start | bytes 6148
  114.4 8.3 %copy-start = (f32[512,256]{1,0:T(8,128)S(1)}, f32[512,256]{1,0:T(8,128)}, u32[]{:S(2)}) copy-start(f32[512,256]{1,0:T(8,128)} %get-tuple-element.19) | copy-start | bytes 1572868
  114.4 9.1 %copy-start.1 = (f32[256,256]{1,0:T(8,128)S(1)}, f32[256,256]{1,0:T(8,128)}, u32[]{:S(2)}) copy-start(f32[256,256]{1,0:T(8,128)} %get-tuple-element.20) | copy-start | bytes 786436

commit v2 on v1

--- a/solution.py
+++ b/solution.py
@@ -29,12 +29,12 @@
 
 def body(
     D, N, H,
-    feats, w1, w2, fresh, bank, bias, dest,
+    feats, w1, w2, fresh, bank, lists, dest,
     loss_out, gf_out, gs_out, keys_out, kd_out,
     hid, zp, zr, zs, zfull, kcat, qcat, sbuf, acc, ml, ar, mr, st, gz, gfull, lt, lr,
-    gfs, gfr, gsp, gsr, gst, gsf, ks, kr, kd, kdr,
+    gfs, gfr, gfl, gsp, gsr, gst, gsf, ks, kr, kd, kdr,
     s_z, r_z, s_q, r_q, s_a, r_a, s_m, r_m, s_g, r_g, s_l, r_l,
-    s_f, r_f, s_s, r_s, s_t, r_t, s_k, r_k, s_d, r_d,
+    s_f, r_f, s_s, r_s, s_t, r_t, s_k, r_k, s_d, r_d, s_fl, r_fl, bvm, s_b,
 ):
     d = lax.axis_index("dp")
     bk = lax.axis_index("bank")
@@ -62,6 +62,12 @@
         c.start()
         return c
 
+    def load(b):
+        at = pl.ds(pl.multiple_of(b * BLOCK, BLOCK), BLOCK)
+        return pltpu.make_async_copy(bank.at[at], bvm.at[at], s_b.at[b])
+
+    for b in range(nblk):
+        load(b).start()
     barrier = pltpu.get_barrier_semaphore()
     for k in range(1, N):
         pl.semaphore_signal(barrier, inc=1, device_id=plane(k)[1], device_id_type=MESH)
@@ -81,7 +87,7 @@
 
     f = fresh[...]
     unit = f / jnp.sqrt(jnp.sum(f * f, axis=1, keepdims=True) + EPS)
-    local = dest[...] - (me * bank.shape[0]).astype(F32)
+    local = jnp.broadcast_to(dest[...].astype(F32), (8, rows)) - (me * bank.shape[0]).astype(F32)
     inside = (local >= 0.0) & (local < float(bank.shape[0]))
     one = jnp.where(inside, 1.0, 0.0)
     upper = lax.broadcasted_iota(jnp.int32, (rows, rows), 0) <= lax.broadcasted_iota(
@@ -100,7 +106,8 @@
     kdr[0] = kd[...]
 
     def split(b, carry):
-        x = bank[pl.ds(pl.multiple_of(b * BLOCK, BLOCK), BLOCK), :]
+        load(b).wait()
+        x = bvm[pl.ds(pl.multiple_of(b * BLOCK, BLOCK), BLOCK), :]
         hi = x.astype(BF16)
         lo = (x - hi.astype(F32)).astype(BF16)
         kcat[b, :, 0:256] = hi
@@ -130,7 +137,8 @@
     qcat[:, 512:768] = (q - qh.astype(F32)).astype(BF16)
 
     def scores(b, best):
-        s = nt(qcat[...], kcat[b]) + bias[b]
+        hit = jnp.max(jnp.where(lists[...] == me * nblk + b, 0.0, LOWEST), axis=1, keepdims=True)
+        s = nt(qcat[...], kcat[b]) + hit
         sbuf[b] = s
         for t in range(BLOCK // 128):
             best = jnp.maximum(best, s[:, t * 128:(t + 1) * 128])
@@ -212,27 +220,56 @@
     gp = nt(gb, w2[...])
     gp = jnp.where(hid[...] > 0, gp, 0.0).astype(BF16)
     F = gf_out.shape[0]
-    f_copies = []
     if F % 128:
         for t in range(feats.shape[1] // 256):
             gfs[t * 256:(t + 1) * 256, :] = tn(feats[:, t * 256:(t + 1) * 256], gp)
-    for j in [*range(1, D), 0]:
-        p, dev = line(j)
+
+    def hop(p, nxt, got, ss, rs):
+        return pltpu.make_async_remote_copy(
+            src_ref=gfs.at[chunk(p, F)], dst_ref=got.at[p], send_sem=ss.at[p],
+            recv_sem=rs.at[p], device_id={"dp": nxt}, device_id_type=MESH)
+
+    def step(p, first, nxt, got, ss, rs):
         if F % 128 == 0:
             gfs[chunk(p, F), :] = tn(feats[:, chunk(p, F)], gp)
-        if j:
-            f_copies.append(send(gfs.at[chunk(p, F)], gfr.at[j], s_f.at[j], r_f.at[j], dev))
-
-    total_s = gsp[chunk(d, S), :]
-    for j in range(1, D):
-        s_copies[j - 1].wait_recv()
-        total_s = total_s + gsr[j]
-    gst[...] = total_s
-    gsf[chunk(d, S), :] = total_s
+        move = hop(p, nxt, got, ss, rs)
+
+        @pl.when(jnp.logical_not(first))
+        def _():
+            move.wait_recv()
+            gfs[chunk(p, F), :] += got[p]
+
+        move.start()
+
+    up = lax.min(d + 1, D - 1)
+    down = lax.max(d - 1, 0)
+
+    def both_ways(t, act):
+        @pl.when(d <= t)
+        def _():
+            act(D - 1 - t + d, d == 0, up, gfr, s_f, r_f)
+
+        @pl.when(d >= D - 1 - t)
+        def _():
+            act(t - (D - 1 - d), d == D - 1, down, gfl, s_fl, r_fl)
+
     t_copies = []
-    for j in range(1, D):
-        dev = line(j)[1]
-        t_copies.append(send(gst, gsf.at[chunk(d, S)], s_t.at[j], r_t.at[j], dev))
+    for t in range(D - 1):
+        both_ways(t, step)
+        if t == 0:
+            total_s = gsp[chunk(d, S), :]
+            for j in range(1, D):
+                s_copies[j - 1].wait_recv()
+                total_s = total_s + gsr[j]
+            gst[...] = total_s
+            gsf[chunk(d, S), :] = total_s
+            for j in range(1, D):
+                dev = line(j)[1]
+                t_copies.append(send(gst, gsf.at[chunk(d, S)], s_t.at[j], r_t.at[j], dev))
+    if F % 128 == 0:
+        gf_out[...] = tn(feats[:, chunk(d, F)], gp)
+    else:
+        gf_out[...] = gfs[chunk(d, F), :]
 
     for c in pending:
         c.wait_recv()
@@ -242,16 +279,40 @@
     for c in t_copies:
         c.wait_recv()
     gs_out[...] = gsf[...]
-    gf_out[...] = gfs[chunk(d, F), :]
-    for j in range(1, D):
-        f_copies[j - 1].wait_recv()
-        gf_out[...] += gfr[j]
-    for c in z_copies + q_copies + a_copies + g_copies + s_copies + t_copies + f_copies + pending:
+
+    @pl.when(d > 0)
+    def _():
+        hop(d, up, gfr, s_f, r_f).wait_recv()
+        gf_out[...] += gfr[d]
+
+    @pl.when(d < D - 1)
+    def _():
+        hop(d, down, gfl, s_fl, r_fl).wait_recv()
+        gf_out[...] += gfl[d]
+
+    for t in range(D - 1):
+        both_ways(t, lambda p, first, nxt, got, ss, rs: hop(p, nxt, got, ss, rs).wait_send())
+    for c in z_copies + q_copies + a_copies + g_copies + s_copies + t_copies + pending:
         c.wait_send()
 
 
+def place_rows(D, R, bank, keys, where, out, sem):
+    copy = pltpu.make_async_copy(bank, out, sem)
+    copy.start()
+    copy.wait()
+
+    def group(i, carry):
+        j = lax.div(i, R // 8)
+        first = lax.rem(i, R // 8) * 8
+        for t in range(8):
+            row = (where[j, 0, first + t] + 0.5).astype(jnp.int32)
+            out[pl.ds(row, 1), :] = keys[pl.ds(i * 8 + t, 1), :]
+        return carry
+
+    lax.fori_loop(0, D * R // 8, group, 0)
+
+
 def shards(D, N, H, feats, w_first, w_second, fresh_keys, bank, block_lists, dest_rows):
-    owner = lax.axis_index(("bank", "head"))
     rows, din = feats.shape
     hcols = w_first.shape[1]
     E = w_second.shape[1]
@@ -259,11 +320,8 @@
     R = rows // N
     F = din // D
     S = hcols // D
-    mine = owner * nblk + jnp.arange(nblk, dtype=jnp.int32)
-    owned = jnp.any(block_lists[0][None, :] == mine[:, None], axis=1)
-    bias = jnp.where(owned, 0.0, LOWEST).astype(F32)
-    dest = jnp.broadcast_to(dest_rows.astype(F32)[None, :], (8, rows))
     V = pl.BlockSpec(memory_space=pltpu.VMEM)
+    ANY = pl.BlockSpec(memory_space=pl.ANY)
     sds = jax.ShapeDtypeStruct
     vm = pltpu.VMEM
     scratch = [
@@ -272,26 +330,32 @@
         vm((nblk, rows, BLOCK), F32), vm((rows, E), F32), vm((rows // 128, 8, 128), F32),
         vm((N, R, E), F32), vm((N, 8, 128), F32), vm((128, 128), F32), vm((R, E), F32),
         vm((rows, E), F32), vm((8, 128), F32), vm((N, 8, 128), F32),
-        vm((din, hcols), F32), vm((D, F, hcols), F32), vm((hcols, E), F32), vm((D, S, E), F32),
+        vm((din, hcols), F32), vm((D, F, hcols), F32), vm((D, F, hcols), F32), vm((hcols, E), F32), vm((D, S, E), F32),
         vm((S, E), F32), vm((hcols, E), F32), vm((R, E), F32), vm((D, R, E), F32),
         vm((8, 128), F32), vm((D, 8, 128), F32),
     ]
     dma = pltpu.SemaphoreType.DMA
-    sems = [dma((N,))] * 12 + [dma((D,))] * 10
+    sems = [dma((N,))] * 12 + [dma((D,))] * 12 + [vm(bank.shape, F32), dma((nblk,))]
     loss, grad_first, grad_second, keys, kdest = pl.pallas_call(
         functools.partial(body, D, N, H),
         out_shape=(
             sds((N, 8, 128), F32), sds((F, hcols), F32), sds((hcols, E), F32),
             sds((D * R, E), F32), sds((D, 8, 128), F32),
         ),
-        in_specs=[V, V, V, V, V, pl.BlockSpec(memory_space=pltpu.SMEM), V],
+        in_specs=[V, V, V, V, ANY, V, V],
         out_specs=(V,) * 5,
         scratch_shapes=scratch + sems,
         compiler_params=pltpu.CompilerParams(
             collective_id=0, has_side_effects=True, vmem_limit_bytes=56 * 1024 * 1024),
-    )(feats, w_first, w_second, fresh_keys, bank, bias, dest)
-    index = jnp.round(kdest[:, 0, :R]).astype(jnp.int32).reshape(D * R)
-    new_bank = bank.at[index].set(keys, unique_indices=True, mode="promise_in_bounds")
+    )(feats, w_first, w_second, fresh_keys, bank, block_lists, dest_rows.reshape(1, rows))
+    new_bank = pl.pallas_call(
+        functools.partial(place_rows, D, R),
+        out_shape=sds(bank.shape, F32),
+        in_specs=[ANY, V, pl.BlockSpec(memory_space=pltpu.SMEM)],
+        out_specs=V,
+        scratch_shapes=[dma],
+        compiler_params=pltpu.CompilerParams(vmem_limit_bytes=16 * 1024 * 1024),
+    )(bank, keys, kdest)
     return (loss[:, 0, :R].reshape(rows), grad_first, grad_second, new_bank)
 
 

time: 125 us -> 109 us (0.87)
  local copies, waits for them, and re-layouts: 14.2 us -> 6.79 us
  Pallas kernels: 108 us -> 101 us
  other arithmetic: 1.45 us -> 0 us
    pallas_call x1, Pallas kernels: 108 us -> 96.4 us  [shards(): pl.pallas_call(functools.partial(body, D, N, H), out_shape=(sds((N, 8, 12...]
    scatter x1 -> x0, local copies, waits for them, and re-layouts: 5.98 us -> none  [shards(): bank.at[index].set(keys, unique_indices=True, mode='promise_in_bounds')]
    pallas_call x0 -> x1, Pallas kernels: none -> 4.9 us  [shards(): pl.pallas_call(functools.partial(place_rows, D, R), out_shape=sds(bank.sh...]
    unnamed x11 -> x12, local copies, waits for them, and re-layouts: 5.99 us -> 5.36 us
where the time goes in v2:
time: 109 us
  Pallas kernels  101 us (93%)
  local copies, waits for them, and re-layouts  6.79 us (6%)
    pallas_call x1, Pallas kernels, shards(): pl.pallas_call(functools.partial(body, D, N, H), out_shape=(sds((N, 8, 12...  96.4 us
    unnamed x12, local copies, waits for them, and re-layouts  5.36 us
    pallas_call x1, Pallas kernels, shards(): pl.pallas_call(functools.partial(place_rows, D, R), out_shape=sds(bank.sh...  4.9 us

profile of v2, /device:TPU:0, one launch (start us, length us, event | category | flops | bytes accessed | tf_op | source)
XLA Modules:
  0.0 108.7 jit_solution(4096895930665945059)
XLA Ops:
  0.6 96.4 %shard_map.102 = (f32[8,8,128]{2,1,0:T(8,128)}, f32[512,256]{1,0:T(8,128)}, f32[256,256]{1,0:T(8,128)}, f32[256,256]{1,0:T(8,128)}, f32[4,8,128]{2,1,0:T(8,128)}) custom-call(bf16[512,2048]{1,0:T(8,128)(2,1)} %feats.1, bf16[2048,256]{1,0:T(8,128)(2,1)} %w1.1, bf16[256,256]{1,0:T(8,128)(2,1)} %w2.1, f32[512,256]{1,0:T(8,128)} %fresh.1, f32[4096,256]{1,0:T(8,128)} %bank.3, ...), custom_call_target="tpu_custom_call" | custom-call | tf_op jit(solution)/shard_map/pallas_call | solution.py:339
  97.0 0.8 slice_reduce_fusion
  97.8 0.7 reshape_squeeze.3
  98.4 0.0 copy-start
  98.4 2.2 %copy-done = f32[4096,256]{1,0:T(8,128)S(1)} copy-done((f32[4096,256]{1,0:T(8,128)S(1)}, f32[4096,256]{1,0:T(8,128)}, u32[]{:S(2)}) %copy-start) | copy-done | bytes 4194328
  100.6 0.0 copy-start.1
  100.6 0.9 copy-done.1
  101.6 0.0 copy-start.2
  101.6 0.7 copy-done.2
  102.3 0.0 copy-start.3
  102.3 0.0 copy-start.4
  102.3 4.9 %shard_map.103 = f32[4096,256]{1,0:T(8,128)} custom-call(f32[4096,256]{1,0:T(8,128)S(1)} %copy-done, f32[256,256]{1,0:T(8,128)S(1)} %copy-done.1, f32[4,8,128]{2,1,0:T(8,128)S(1)} %copy-done.2), custom_call_target="tpu_custom_call" | custom-call | tf_op jit(solution)/shard_map/pallas_call | solution.py:351
  107.2 0.0 copy-done.3
  107.2 0.8 copy.13
  108.0 0.0 copy-done.4
  108.0 0.7 copy.14
Async XLA Ops:
  98.4 2.2 %copy-start = (f32[4096,256]{1,0:T(8,128)S(1)}, f32[4096,256]{1,0:T(8,128)}, u32[]{:S(2)}) copy-start(f32[4096,256]{1,0:T(8,128)} %bank.3) | copy-start | bytes 12582916
  100.6 0.9 copy-start.1
  101.6 0.7 copy-start.2
  102.3 4.9 %copy-start.3 = (f32[512,256]{1,0:T(8,128)S(1)}, f32[512,256]{1,0:T(8,128)}, u32[]{:S(2)}) copy-start(f32[512,256]{1,0:T(8,128)} %get-tuple-element.19) | copy-start | bytes 1572868
  102.3 5.7 %copy-start.4 = (f32[256,256]{1,0:T(8,128)S(1)}, f32[256,256]{1,0:T(8,128)}, u32[]{:S(2)}) copy-start(f32[256,256]{1,0:T(8,128)} %get-tuple-element.20) | copy-start | bytes 786436

commit v3 on v2

--- a/solution.py
+++ b/solution.py
@@ -30,11 +30,11 @@
 def body(
     D, N, H,
     feats, w1, w2, fresh, bank, lists, dest,
-    loss_out, gf_out, gs_out, keys_out, kd_out,
+    loss_out, gf_out, gs_out, bank_out,
     hid, zp, zr, zs, zfull, kcat, qcat, sbuf, acc, ml, ar, mr, st, gz, gfull, lt, lr,
     gfs, gfr, gfl, gsp, gsr, gst, gsf, ks, kr, kd, kdr,
     s_z, r_z, s_q, r_q, s_a, r_a, s_m, r_m, s_g, r_g, s_l, r_l,
-    s_f, r_f, s_s, r_s, s_t, r_t, s_k, r_k, s_d, r_d, s_fl, r_fl, bvm, s_b,
+    s_f, r_f, s_s, r_s, s_t, r_t, s_k, r_k, s_d, r_d, s_fl, r_fl, bvm, s_b, s_o, k3,
 ):
     d = lax.axis_index("dp")
     bk = lax.axis_index("bank")
@@ -68,6 +68,24 @@
 
     for b in range(nblk):
         load(b).start()
+    C = N // H
+    sibling = {"head": 1 - hd}
+
+    def gather_rows(mine, full, ss, rs):
+        at = full.at[chunk(me, R)]
+        away = []
+        for i in range(1, C):
+            dev = {"bank": lax.rem(bk + i, C)}
+            away.append(send(mine, at, ss.at[i], rs.at[i], dev))
+        near = [send(mine, at, ss.at[C], rs.at[C], sibling)]
+        for i in range(1, C):
+            away[i - 1].wait_recv()
+            came = full.at[chunk(lax.rem(bk + C - i, C) * H + hd, R)]
+            near.append(send(came, came, ss.at[C + i], rs.at[C + i], sibling))
+        for c in near:
+            c.wait_recv()
+        return away + near
+
     barrier = pltpu.get_barrier_semaphore()
     for k in range(1, N):
         pl.semaphore_signal(barrier, inc=1, device_id=plane(k)[1], device_id_type=MESH)
@@ -97,7 +115,8 @@
     want = lax.broadcasted_iota(jnp.int32, (128, rows), 0).astype(F32) + 1.0
     pick = jnp.where(want == jnp.broadcast_to(place[0:1, :], (128, rows)), 1.0, 0.0)
     ks[...] = jnp.dot(pick[0:R], unit, precision=lax.Precision.HIGHEST, preferred_element_type=F32)
-    kd[...] = nt(jnp.where(inside, local, 0.0), pick, precision=lax.Precision.HIGHEST)
+    spots = nt(jnp.where(inside, local, 0.0), pick, precision=lax.Precision.HIGHEST)
+    kd[...] = jnp.floor(spots + 0.5)
     for j in range(1, D):
         dev = line(j)[1]
         pending.append(send(ks, kr.at[j], s_k.at[j], r_k.at[j], dev))
@@ -123,12 +142,7 @@
         total_z = total_z + zr[k]
     zs[...] = total_z
     zfull[chunk(me, R), :] = total_z
-    q_copies = []
-    for k in range(1, N):
-        dev = plane(k)[1]
-        q_copies.append(send(zs, zfull.at[chunk(me, R)], s_q.at[k], r_q.at[k], dev))
-    for c in q_copies:
-        c.wait_recv()
+    q_copies = gather_rows(zs, zfull, s_q, r_q)
     z = zfull[...]
     q = z / jnp.sqrt(jnp.sum(z * z, axis=1, keepdims=True) + EPS) * (SCALE * LOG2E)
     qh = q.astype(BF16)
@@ -202,13 +216,9 @@
         [jnp.broadcast_to(losses, (R, 128)), jnp.zeros((128 - R, 128), F32)], axis=0)
     lt[...] = wide.T[0:8, :]
     lr[me] = lt[...]
-    g_copies = []
-    for k in range(1, N):
-        dev = plane(k)[1]
-        g_copies.append(send(gz, gfull.at[chunk(me, R)], s_g.at[k], r_g.at[k], dev))
-        pending.append(send(lt, lr.at[me], s_l.at[k], r_l.at[k], dev))
-    for c in g_copies:
-        c.wait_recv()
+    for k in range(1, N):
+        pending.append(send(lt, lr.at[me], s_l.at[k], r_l.at[k], plane(k)[1]))
+    g_copies = gather_rows(gz, gfull, s_g, r_g)
 
     gb = gfull[...].astype(BF16)
     gsp[...] = tn(hid[...], gb)
@@ -273,8 +283,31 @@
 
     for c in pending:
         c.wait_recv()
-    keys_out[...] = kr[...].reshape(keys_out.shape)
-    kd_out[...] = kdr[...]
+    spot = jnp.concatenate([kdr[j][0:1, 0:R] for j in range(D)], axis=1)
+    k = kr[...].reshape(D * R, kr.shape[2])
+    k_hi = k.astype(BF16)
+    k = k - k_hi.astype(F32)
+    k_mid = k.astype(BF16)
+    k3[:, 0:256] = k_hi
+    k3[:, 256:512] = k_mid
+    k3[:, 512:768] = (k - k_mid.astype(F32)).astype(BF16)
+
+    def store(b):
+        at = pl.ds(pl.multiple_of(b * BLOCK, BLOCK), BLOCK)
+        return pltpu.make_async_copy(bvm.at[at], bank_out.at[at], s_o.at[b])
+
+    def place_block(b, carry):
+        row = (lax.broadcasted_iota(jnp.int32, (BLOCK, D * R), 0) + b * BLOCK).astype(F32)
+        one_hot = jnp.where(row == spot, 1.0, 0.0)
+        new = jnp.dot(one_hot.astype(BF16), k3[...], preferred_element_type=F32)
+        new = new[:, 0:256] + new[:, 256:512] + new[:, 512:768]
+        hit = jnp.max(one_hot, axis=1, keepdims=True) > 0.0
+        at = pl.ds(pl.multiple_of(b * BLOCK, BLOCK), BLOCK)
+        bvm[at, :] = jnp.where(hit, new, bvm[at, :])
+        store(b).start()
+        return carry
+
+    lax.fori_loop(0, nblk, place_block, 0)
     loss_out[...] = lr[...]
     for c in t_copies:
         c.wait_recv()
@@ -290,26 +323,12 @@
         hop(d, down, gfl, s_fl, r_fl).wait_recv()
         gf_out[...] += gfl[d]
 
+    for b in range(nblk):
+        store(b).wait()
     for t in range(D - 1):
         both_ways(t, lambda p, first, nxt, got, ss, rs: hop(p, nxt, got, ss, rs).wait_send())
     for c in z_copies + q_copies + a_copies + g_copies + s_copies + t_copies + pending:
         c.wait_send()
-
-
-def place_rows(D, R, bank, keys, where, out, sem):
-    copy = pltpu.make_async_copy(bank, out, sem)
-    copy.start()
-    copy.wait()
-
-    def group(i, carry):
-        j = lax.div(i, R // 8)
-        first = lax.rem(i, R // 8) * 8
-        for t in range(8):
-            row = (where[j, 0, first + t] + 0.5).astype(jnp.int32)
-            out[pl.ds(row, 1), :] = keys[pl.ds(i * 8 + t, 1), :]
-        return carry
-
-    lax.fori_loop(0, D * R // 8, group, 0)
 
 
 def shards(D, N, H, feats, w_first, w_second, fresh_keys, bank, block_lists, dest_rows):
@@ -335,27 +354,19 @@
         vm((8, 128), F32), vm((D, 8, 128), F32),
     ]
     dma = pltpu.SemaphoreType.DMA
-    sems = [dma((N,))] * 12 + [dma((D,))] * 12 + [vm(bank.shape, F32), dma((nblk,))]
-    loss, grad_first, grad_second, keys, kdest = pl.pallas_call(
+    sems = [dma((N,))] * 12 + [dma((D,))] * 12 + [vm(bank.shape, F32), dma((nblk,)), dma((nblk,)), vm((D * R, 3 * E), BF16)]
+    loss, grad_first, grad_second, new_bank = pl.pallas_call(
         functools.partial(body, D, N, H),
         out_shape=(
             sds((N, 8, 128), F32), sds((F, hcols), F32), sds((hcols, E), F32),
-            sds((D * R, E), F32), sds((D, 8, 128), F32),
+            sds(bank.shape, F32),
         ),
         in_specs=[V, V, V, V, ANY, V, V],
-        out_specs=(V,) * 5,
+        out_specs=(V, V, V, ANY),
         scratch_shapes=scratch + sems,
         compiler_params=pltpu.CompilerParams(
             collective_id=0, has_side_effects=True, vmem_limit_bytes=56 * 1024 * 1024),
     )(feats, w_first, w_second, fresh_keys, bank, block_lists, dest_rows.reshape(1, rows))
-    new_bank = pl.pallas_call(
-        functools.partial(place_rows, D, R),
-        out_shape=sds(bank.shape, F32),
-        in_specs=[ANY, V, pl.BlockSpec(memory_space=pltpu.SMEM)],
-        out_specs=V,
-        scratch_shapes=[dma],
-        compiler_params=pltpu.CompilerParams(vmem_limit_bytes=16 * 1024 * 1024),
-    )(bank, keys, kdest)
     return (loss[:, 0, :R].reshape(rows), grad_first, grad_second, new_bank)
 
 

time: 109 us -> 104 us (0.954)
  Pallas kernels: 101 us -> 93.4 us
  local copies, waits for them, and re-layouts: 6.79 us -> 9.43 us
    pallas_call x1 -> x0, Pallas kernels: 4.9 us -> none  [shards(): pl.pallas_call(functools.partial(place_rows, D, R), out_shape=sds(bank.sh...]
    pallas_call x1, Pallas kernels: 96.4 us -> 93.4 us  [shards(): pl.pallas_call(functools.partial(body, D, N, H), out_shape=(sds((N, 8, 12...]
    unnamed x12 -> x3, local copies, waits for them, and re-layouts: 5.36 us -> 8.01 us
where the time goes in v3:
time: 104 us
  Pallas kernels  93.4 us (90%)
  local copies, waits for them, and re-layouts  9.43 us (9%)
    pallas_call x1, Pallas kernels, shards(): pl.pallas_call(functools.partial(body, D, N, H), out_shape=(sds((N, 8, 12...  93.4 us
    unnamed x3, local copies, waits for them, and re-layouts  8.01 us

profile of v3, /device:TPU:0, one launch (start us, length us, event | category | flops | bytes accessed | tf_op | source)
XLA Modules:
  0.0 103.5 jit_solution(16128723558506283903)
XLA Ops:
  0.6 93.4 %shard_map.102 = (f32[8,8,128]{2,1,0:T(8,128)}, f32[512,256]{1,0:T(8,128)}, f32[256,256]{1,0:T(8,128)}, f32[4096,256]{1,0:T(8,128)}) custom-call(bf16[512,2048]{1,0:T(8,128)(2,1)} %feats.1, bf16[2048,256]{1,0:T(8,128)(2,1)} %w1.1, bf16[256,256]{1,0:T(8,128)(2,1)} %w2.1, f32[512,256]{1,0:T(8,128)} %fresh.1, f32[4096,256]{1,0:T(8,128)} %bank.1, ...), custom_call_target="tpu_custom_call" | custom-call | tf_op jit(solution)/shard_map/pallas_call | solution.py:358
  94.1 0.8 slice_reduce_fusion
  94.8 0.7 reshape_squeeze.3
  95.5 1.9 %copy.14 = f32[512,256]{1,0:T(8,128)} copy(f32[512,256]{1,0:T(8,128)} %get-tuple-element.17) | data formatting | bytes 1048576
  97.4 1.7 %copy.15 = f32[256,256]{1,0:T(8,128)} copy(f32[256,256]{1,0:T(8,128)} %get-tuple-element.18) | data formatting | bytes 524288
  99.0 4.5 %copy.16 = f32[4096,256]{1,0:T(8,128)} copy(f32[4096,256]{1,0:T(8,128)} %get-tuple-element.19) | data formatting | bytes 8388608

commit v4 on v3

--- a/solution.py
+++ b/solution.py
@@ -34,7 +34,7 @@
     hid, zp, zr, zs, zfull, kcat, qcat, sbuf, acc, ml, ar, mr, st, gz, gfull, lt, lr,
     gfs, gfr, gfl, gsp, gsr, gst, gsf, ks, kr, kd, kdr,
     s_z, r_z, s_q, r_q, s_a, r_a, s_m, r_m, s_g, r_g, s_l, r_l,
-    s_f, r_f, s_s, r_s, s_t, r_t, s_k, r_k, s_d, r_d, s_fl, r_fl, bvm, s_b, s_o, k3,
+    s_f, r_f, s_s, r_s, s_t, r_t, s_k, r_k, s_d, r_d, s_fl, r_fl, bvm, s_b, s_o, k3, zh,
 ):
     d = lax.axis_index("dp")
     bk = lax.axis_index("bank")
@@ -99,9 +99,17 @@
 
     pending = []
     z_copies = []
-    for k in range(1, N):
-        p, dev = plane(k)
-        z_copies.append(send(zp.at[chunk(p, R)], zr.at[k], s_z.at[k], r_z.at[k], dev))
+    turns = [*range(1, C), 0]
+    for i in turns:
+        part = zp.at[chunk(lax.rem(bk + i, C) * H + 1 - hd, R)]
+        z_copies.append(send(part, zr.at[i], s_z.at[i], r_z.at[i], sibling))
+    z_away = []
+    for i in turns:
+        z_copies[turns.index(i)].wait_recv()
+        c = lax.rem(bk + i, C)
+        zh[i] = zp[chunk(c * H + hd, R), :] + zr[i]
+        if i:
+            z_away.append(send(zh.at[i], zr.at[C + i], s_z.at[C + i], r_z.at[C + i], {"bank": c}))
 
     f = fresh[...]
     unit = f / jnp.sqrt(jnp.sum(f * f, axis=1, keepdims=True) + EPS)
@@ -136,10 +144,10 @@
 
     lax.fori_loop(0, nblk, split, 0)
 
-    total_z = zp[chunk(me, R), :]
-    for k in range(1, N):
-        z_copies[k - 1].wait_recv()
-        total_z = total_z + zr[k]
+    total_z = zh[0]
+    for i in range(1, C):
+        z_away[i - 1].wait_recv()
+        total_z = total_z + zr[C + i]
     zs[...] = total_z
     zfull[chunk(me, R), :] = total_z
     q_copies = gather_rows(zs, zfull, s_q, r_q)
@@ -327,8 +335,23 @@
         store(b).wait()
     for t in range(D - 1):
         both_ways(t, lambda p, first, nxt, got, ss, rs: hop(p, nxt, got, ss, rs).wait_send())
-    for c in z_copies + q_copies + a_copies + g_copies + s_copies + t_copies + pending:
+    for c in z_copies + z_away + q_copies + a_copies + g_copies + s_copies + t_copies + pending:
         c.wait_send()
+
+
+def hand_on(gf, gs, bank, gf_out, gs_out, bank_out, sems):
+    size = bank.shape[0] // 8
+    copies = [
+        pltpu.make_async_copy(
+            bank.at[i * size:(i + 1) * size], bank_out.at[i * size:(i + 1) * size], sems.at[i])
+        for i in range(8)
+    ]
+    copies.append(pltpu.make_async_copy(gf, gf_out, sems.at[8]))
+    copies.append(pltpu.make_async_copy(gs, gs_out, sems.at[9]))
+    for c in copies:
+        c.start()
+    for c in copies:
+        c.wait()
 
 
 def shards(D, N, H, feats, w_first, w_second, fresh_keys, bank, block_lists, dest_rows):
@@ -354,7 +377,7 @@
         vm((8, 128), F32), vm((D, 8, 128), F32),
     ]
     dma = pltpu.SemaphoreType.DMA
-    sems = [dma((N,))] * 12 + [dma((D,))] * 12 + [vm(bank.shape, F32), dma((nblk,)), dma((nblk,)), vm((D * R, 3 * E), BF16)]
+    sems = [dma((N,))] * 12 + [dma((D,))] * 12 + [vm(bank.shape, F32), dma((nblk,)), dma((nblk,)), vm((D * R, 3 * E), BF16), vm((N // H, R, E), F32)]
     loss, grad_first, grad_second, new_bank = pl.pallas_call(
         functools.partial(body, D, N, H),
         out_shape=(
@@ -367,6 +390,15 @@
         compiler_params=pltpu.CompilerParams(
             collective_id=0, has_side_effects=True, vmem_limit_bytes=56 * 1024 * 1024),
     )(feats, w_first, w_second, fresh_keys, bank, block_lists, dest_rows.reshape(1, rows))
+    results = (grad_first, grad_second, new_bank)
+    grad_first, grad_second, new_bank = pl.pallas_call(
+        hand_on,
+        out_shape=tuple(sds(x.shape, F32) for x in results),
+        in_specs=[ANY] * 3,
+        out_specs=(ANY,) * 3,
+        scratch_shapes=[dma((10,))],
+        compiler_params=pltpu.CompilerParams(vmem_limit_bytes=60 * 1024 * 1024),
+    )(*results)
     return (loss[:, 0, :R].reshape(rows), grad_first, grad_second, new_bank)
 
 

time: 104 us -> 247 us (2.38)
  Pallas kernels: 93.4 us -> 245 us
  local copies, waits for them, and re-layouts: 9.43 us -> 1.43 us
    pallas_call x0 -> x1, Pallas kernels: none -> 152 us  [shards(): pl.pallas_call(hand_on, out_shape=tuple((sds(x.shape, F32) for x in resul...]
    unnamed x3 -> x0, local copies, waits for them, and re-layouts: 8.01 us -> none
where the time goes in v4:
time: 247 us
  Pallas kernels  245 us (99%)
    pallas_call x1, Pallas kernels, shards(): pl.pallas_call(hand_on, out_shape=tuple((sds(x.shape, F32) for x in resul...  152 us
    pallas_call x1, Pallas kernels, shards(): pl.pallas_call(functools.partial(body, D, N, H), out_shape=(sds((N, 8, 12...  92.4 us

profile of v4, /device:TPU:0, one launch (start us, length us, event | category | flops | bytes accessed | tf_op | source)
XLA Modules:
  0.0 246.6 jit_solution(16587818100441250562)
XLA Ops:
  0.6 92.4 %shard_map.102 = (f32[8,8,128]{2,1,0:T(8,128)}, f32[512,256]{1,0:T(8,128)}, f32[256,256]{1,0:T(8,128)}, f32[4096,256]{1,0:T(8,128)}) custom-call(bf16[512,2048]{1,0:T(8,128)(2,1)} %feats.1, bf16[2048,256]{1,0:T(8,128)(2,1)} %w1.1, bf16[256,256]{1,0:T(8,128)(2,1)} %w2.1, f32[512,256]{1,0:T(8,128)} %fresh.1, f32[4096,256]{1,0:T(8,128)} %bank.1, ...), custom_call_target="tpu_custom_call" | custom-call | tf_op jit(solution)/shard_map/pallas_call | solution.py:381
  93.1 0.8 slice_reduce_fusion
  93.9 0.7 reshape_squeeze.3
  94.5 152.1 %shard_map.103 = (f32[512,256]{1,0:T(8,128)}, f32[256,256]{1,0:T(8,128)}, f32[4096,256]{1,0:T(8,128)}) custom-call(f32[512,256]{1,0:T(8,128)} %get-tuple-element.12.gf, f32[256,256]{1,0:T(8,128)} %get-tuple-element.13.gs, f32[4096,256]{1,0:T(8,128)} %get-tuple-element.14.bank), custom_call_target="tpu_custom_call" | custom-call | tf_op jit(solution)/shard_map/pallas_call | solution.py:394

commit v5 on v4

--- a/solution.py
+++ b/solution.py
@@ -339,18 +339,20 @@
         c.wait_send()
 
 
-def hand_on(gf, gs, bank, gf_out, gs_out, bank_out, sems):
+def hand_on(gf, gs, bank, gf_out, gs_out, bank_out, gf_buf, gs_buf, bank_buf, got, put):
     size = bank.shape[0] // 8
-    copies = [
-        pltpu.make_async_copy(
-            bank.at[i * size:(i + 1) * size], bank_out.at[i * size:(i + 1) * size], sems.at[i])
-        for i in range(8)
-    ]
-    copies.append(pltpu.make_async_copy(gf, gf_out, sems.at[8]))
-    copies.append(pltpu.make_async_copy(gs, gs_out, sems.at[9]))
-    for c in copies:
+    parts = [(gf, gf_buf, gf_out), (gs, gs_buf, gs_out)]
+    for i in range(8):
+        at = pl.ds(i * size, size)
+        parts.append((bank.at[at], bank_buf.at[at], bank_out.at[at]))
+    reads = [pltpu.make_async_copy(p[0], p[1], got.at[i]) for i, p in enumerate(parts)]
+    writes = [pltpu.make_async_copy(p[1], p[2], put.at[i]) for i, p in enumerate(parts)]
+    for c in reads:
         c.start()
-    for c in copies:
+    for r, w in zip(reads, writes):
+        r.wait()
+        w.start()
+    for c in writes:
         c.wait()
 
 
@@ -396,7 +398,7 @@
         out_shape=tuple(sds(x.shape, F32) for x in results),
         in_specs=[ANY] * 3,
         out_specs=(ANY,) * 3,
-        scratch_shapes=[dma((10,))],
+        scratch_shapes=[vm(x.shape, F32) for x in results] + [dma((10,)), dma((10,))],
         compiler_params=pltpu.CompilerParams(vmem_limit_bytes=60 * 1024 * 1024),
     )(*results)
     return (loss[:, 0, :R].reshape(rows), grad_first, grad_second, new_bank)

time: 247 us -> 99.2 us (0.40)
  Pallas kernels: 245 us -> 96.9 us
    pallas_call x1, Pallas kernels: 152 us -> 4.44 us  [shards(): pl.pallas_call(hand_on, out_shape=tuple((sds(x.shape, F32) for x in resul...]
where the time goes in v5:
time: 99.2 us; the launch traced here: 99 us
  Pallas kernels  96.9 us (98%)
  local copies, waits for them, and re-layouts  1.43 us (1%)
    pallas_call x1, Pallas kernels, shards(): pl.pallas_call(functools.partial(body, D, N, H), out_shape=(sds((N, 8, 12...  92.4 us
    pallas_call x1, Pallas kernels, shards(): pl.pallas_call(hand_on, out_shape=tuple((sds(x.shape, F32) for x in resul...  4.44 us

profile of v5, /device:TPU:0, one launch (start us, length us, event | category | flops | bytes accessed | tf_op | source)
XLA Modules:
  0.0 99.0 jit_solution(4577389468744363686)
XLA Ops:
  0.6 92.4 %shard_map.102 = (f32[8,8,128]{2,1,0:T(8,128)}, f32[512,256]{1,0:T(8,128)}, f32[256,256]{1,0:T(8,128)}, f32[4096,256]{1,0:T(8,128)}) custom-call(bf16[512,2048]{1,0:T(8,128)(2,1)} %feats.1, bf16[2048,256]{1,0:T(8,128)(2,1)} %w1.1, bf16[256,256]{1,0:T(8,128)(2,1)} %w2.1, f32[512,256]{1,0:T(8,128)} %fresh.1, f32[4096,256]{1,0:T(8,128)} %bank.1, ...), custom_call_target="tpu_custom_call" | custom-call | tf_op jit(solution)/shard_map/pallas_call | solution.py:383
  93.1 0.8 slice_reduce_fusion
  93.9 0.7 reshape_squeeze.3
  94.5 4.4 %shard_map.103 = (f32[512,256]{1,0:T(8,128)}, f32[256,256]{1,0:T(8,128)}, f32[4096,256]{1,0:T(8,128)}) custom-call(f32[512,256]{1,0:T(8,128)} %get-tuple-element.12.gf, f32[256,256]{1,0:T(8,128)} %get-tuple-element.13.gs, f32[4096,256]{1,0:T(8,128)} %get-tuple-element.14.bank), custom_call_target="tpu_custom_call" | custom-call | tf_op jit(solution)/shard_map/pallas_call | solution.py:396
